TPU v7x, 32 devices: a whole 2x2x4 slice. The times are simulated.
32 devices in a mesh: groups: 2 (over y), row: 4 (over z), col: 2 (over x), mpo: 2 (over core).
Axes of the slice: x: 2, y: 2, z: 4, core: 2. Of those that a mesh axis runs over, the one named last changes fastest.
Arguments:
- start: float32 [6144, 256], P(('groups', 'row'), 'col'), parts along dimension 0, may hold values from -30 to 30
- left_env: bfloat16 [14, 6144, 256], P('mpo', ('groups', 'row')), parts along dimension 1, may hold values from -1.5 to 3
- right_env: bfloat16 [14, 6144, 256], P('mpo', ('groups', 'row'), 'col'), parts along dimension 1, may hold values from -2.5 to 4
- send_list: int32 [8, 4], P(('groups', 'row')), parts along dimension 0, may hold values from -1 to 2, as said below
- term_source: int32 [24, 14], P(('groups', 'row'), 'mpo'), parts along dimension 0, may hold values from 0 to 6, as said below
- sector_len: int32 [24], P(('groups', 'row')), parts along dimension 0, may hold values from 128 to 256
Outputs:
- residual: float32 [6144, 256], P(('groups', 'row'), 'col'), parts along dimension 0
- coefficients: float32 [10], P('groups'), parts along dimension 0
There are 2 independent parts, one for each index of `groups`. A program takes and returns all parts, laid end to end along the dimension named above; each array names one. Nothing has to cross between parts.
Inputs may be any that keep to these rules, and one draw needn't show every extreme that they name: `send_list`: entry [s, d + c] is -1 where s sends nothing in slot c, and always -1 where s = d. `term_source`: an entry of 3 or more names a slot whose send_list entry is not -1.
All inputs are finite; a program needn't handle non-finite values.
Results may differ from a plain program's by a relative error of at most 0.004.
Values may be sent and summed in bfloat16 or wider, within the bound.
A program may use at most 64 MiB of HBM per device.

v0:
```python
import jax
import jax.numpy as jnp
from jax import lax
from jax.sharding import PartitionSpec as P


def on_device(start, left_env, right_env, send_list, term_source, sector_len):
    sec_dev = sector_len.shape[0]
    k_local = left_env.shape[0]
    width = left_env.shape[2]
    columns = start.shape[1]
    rows_live = jnp.arange(width, dtype=jnp.int32)[None, :] < sector_len[:, None]
    mask = rows_live.astype(jnp.float32).reshape(sec_dev * width, 1)
    left = left_env.reshape(k_local, sec_dev, width, width)
    right = right_env.reshape(k_local, sec_dev, width, columns)
    first = start * mask
    start_sq = lax.psum(jnp.sum(first * first), ("row", "col"))
    vector = first / jnp.sqrt(start_sq + 1e-06)
    previous = jnp.zeros_like(vector)
    beta = jnp.float32(0.0)
    alphas = []
    betas = []
    for step in range(3):
        blocks = vector.astype(jnp.bfloat16).reshape(sec_dev, width, columns)
        pool = lax.all_gather(blocks, "row", axis=0, tiled=True)
        table = lax.all_gather(send_list, "row", axis=0, tiled=True)
        nrows = lax.axis_size("row")
        slot_cap = table.shape[1] // nrows
        mine = lax.axis_index("row")
        offset = jnp.maximum(term_source - sec_dev, 0)
        sender = offset // slot_cap
        which = table[sender, mine * slot_cap + offset % slot_cap]
        remote = sender * sec_dev + jnp.maximum(which, 0)
        lookup = jnp.where(term_source < sec_dev, mine * sec_dev + term_source, remote)
        sources = pool[lookup]
        inner = jnp.einsum(
            "kpab,pkbc->pkac", left, sources, preferred_element_type=jnp.float32
        ).astype(jnp.bfloat16)
        partial_sum = jnp.einsum("pkac,kpdc->pad", inner, right, preferred_element_type=jnp.float32)
        partial_sum = partial_sum.reshape(sec_dev * width, width)
        image = lax.psum_scatter(partial_sum, "col", scatter_dimension=1, tiled=True)
        image = lax.psum(image, "mpo")
        image = image * mask
        alpha = lax.psum(jnp.sum(vector * image), ("row", "col"))
        resid = image - alpha * vector - beta * previous
        resid_sq = None
        if step < 2:
            resid_sq = lax.psum(jnp.sum(resid * resid), ("row", "col"))
        alphas.append(alpha)
        if step < 2:
            beta = jnp.sqrt(resid_sq + 1e-06)
            betas.append(beta)
            previous, vector = (vector, resid / beta)
    return (resid, jnp.stack(alphas + betas))


def solution(mesh):
    placed = (
        P(("groups", "row"), "col"),
        P("mpo", ("groups", "row"), None),
        P("mpo", ("groups", "row"), "col"),
        P(("groups", "row"), None),
        P(("groups", "row"), "mpo"),
        P(("groups", "row")),
    )
    return jax.shard_map(
        on_device,
        mesh=mesh,
        in_specs=placed,
        out_specs=(P(("groups", "row"), "col"), P("groups")),
        check_vma=False,
    )
```

profile of v0, /device:TPU:0, one launch (start us, length us, event | category | flops | bytes accessed | tf_op | source)
XLA Modules:
  0.0 356.8 jit_solution(16965863301647236739)
XLA Ops:
  7.2 0.0 reduce-scatter.4.cloned.1.call-start
  7.3 0.8 shift-left_or_fusion
  8.1 0.1 reshape.56
  8.2 12.7 %all-gather = s32[4,1,4]{2,1,0:T(1,128)S(1)} all-gather(s32[1,1,4]{2,1,0:T(1,128)} %bitcast.55), channel_id=1, replica_groups=mesh['groups'=2,'row'=4,'col'=2,'mpo'=2] {'row'}, dimensions={0}, use_global_device_ids=true | all-gather | bytes 80 | tf_op jit(solution)/shard_map/all_gather | solution.py:26
  20.9 0.8 gather_fusion
  21.7 0.1 reshape.93
  21.8 0.1 reshape.64
  21.9 0.1 fusion.36
  22.0 0.8 multiply_reduce_fusion.5
  22.8 19.3 %psum.63 = f32[]{:T(128)} all-reduce(f32[]{:T(128)} %multiply_reduce_fusion.5), channel_id=1, replica_groups=mesh['groups'=2,'row'=4,'col'=2,'mpo'=2] {'row','col'}, use_global_device_ids=true, to_apply=%region_1.0 | all-reduce | flops 1 | bytes 8 | tf_op jit(solution)/shard_map/psum | solution.py:17
  42.8 0.2 fusion.38
  43.0 18.2 %all_gather.14 = bf16[12,256,128]{2,1,0:T(8,128)(2,1)} all-gather(bf16[3,256,128]{2,1,0:T(8,128)(2,1)S(1)} %bitcast.52), channel_id=1, replica_groups=mesh['groups'=2,'row'=4,'col'=2,'mpo'=2] {'row'}, dimensions={0}, use_global_device_ids=true | all-gather | bytes 983040 | tf_op jit(solution)/shard_map/all_gather | solution.py:25
  61.2 3.0 gather_fusion.1
  64.2 4.0 %fusion.25 = f32[3,256,256,1]{2,1,3,0:T(8,128)} fusion(bf16[3,7,256,128]{3,2,1,0:T(8,128)(2,1)} %bitcast.47, bf16[7,3,256,256]{3,2,1,0:T(8,128)(2,1)S(1)} %bitcast.42, bf16[7,3,256,128]{3,2,1,0:T(8,128)(2,1)} %bitcast.56), kind=kOutput, calls=%fused_computation.16 | convolution fusion | flops 705331200 | bytes 6291456 | tf_op jit(solution)/shard_map/pkac,kpdc->pad/dot_general | solution.py:39
  68.2 0.0 all-reduce.5.cloned.1.call-start
  68.3 15.1 %reduce-scatter.4.cloned.1.call-done = f32[768,128]{1,0:T(8,128)} async-done(((f32[768,256]{1,0:T(8,128)}), f32[768,128]{1,0:T(8,128)}) %reduce-scatter.4.cloned.1.call-update) | async-done | bytes 393232 | tf_op jit(solution)/shard_map/reduce_scatter | solution.py:41
  83.4 0.0 reduce-scatter.6.cloned.1.call-start
  83.4 20.9 %all-reduce.5.cloned.1.call-done = f32[768,128]{1,0:T(8,128)} async-done(((f32[768,128]{1,0:T(8,128)}), f32[768,128]{1,0:T(8,128)}) %all-reduce.5.cloned.1.call-update) | async-done | bytes 393232 | tf_op jit(solution)/shard_map/psum | solution.py:42
  104.4 1.8 multiply_reduce_fusion.4
  106.1 22.3 %psum.65 = f32[]{:T(128)} all-reduce(f32[]{:T(128)} %multiply_reduce_fusion.4), channel_id=1, replica_groups=mesh['groups'=2,'row'=4,'col'=2,'mpo'=2] {'row','col'}, use_global_device_ids=true, to_apply=%region_5.6 | all-reduce | flops 1 | bytes 8 | tf_op jit(solution)/shard_map/psum | solution.py:44
  128.4 2.4 multiply_reduce_fusion.3
  130.8 17.8 %psum.66 = f32[]{:T(128)} all-reduce(f32[]{:T(128)} %multiply_reduce_fusion.3), channel_id=1, replica_groups=mesh['groups'=2,'row'=4,'col'=2,'mpo'=2] {'row','col'}, use_global_device_ids=true, to_apply=%region_7.8 | all-reduce | flops 1 | bytes 8 | tf_op jit(solution)/shard_map/psum | solution.py:48
  149.3 1.8 fusion.39
  151.1 17.1 %all_gather.16 = bf16[12,256,128]{2,1,0:T(8,128)(2,1)} all-gather(bf16[3,256,128]{2,1,0:T(8,128)(2,1)S(1)} %bitcast.54), channel_id=1, replica_groups=mesh['groups'=2,'row'=4,'col'=2,'mpo'=2] {'row'}, dimensions={0}, use_global_device_ids=true | all-gather | bytes 983040 | tf_op jit(solution)/shard_map/all_gather | solution.py:25
  168.3 3.0 gather_fusion.2
  171.3 4.0 %fusion.28 = f32[3,256,256,1]{2,1,3,0:T(8,128)} fusion(bf16[3,7,256,128]{3,2,1,0:T(8,128)(2,1)} %bitcast.48, bf16[7,3,256,256]{3,2,1,0:T(8,128)(2,1)S(1)} %bitcast.44, bf16[7,3,256,128]{3,2,1,0:T(8,128)(2,1)} %bitcast.57), kind=kOutput, calls=%fused_computation.17 | convolution fusion | flops 705331200 | bytes 6291456 | tf_op jit(solution)/shard_map/pkac,kpdc->pad/dot_general | solution.py:39
  175.3 0.0 reduce-scatter.6.cloned.1.call-update
  175.3 0.0 all-reduce.7.cloned.1.call-start
  175.3 16.5 %reduce-scatter.6.cloned.1.call-done = f32[768,128]{1,0:T(8,128)} async-done(((f32[768,256]{1,0:T(8,128)}), f32[768,128]{1,0:T(8,128)}) %reduce-scatter.6.cloned.1.call-update) | async-done | bytes 393232 | tf_op jit(solution)/shard_map/reduce_scatter | solution.py:41
  191.9 0.0 all-reduce.7.cloned.1.call-update
  191.9 0.0 reduce-scatter.8.cloned.1.call-start
  191.9 20.8 %all-reduce.7.cloned.1.call-done = f32[768,128]{1,0:T(8,128)} async-done(((f32[768,128]{1,0:T(8,128)}), f32[768,128]{1,0:T(8,128)}) %all-reduce.7.cloned.1.call-update) | async-done | bytes 393232 | tf_op jit(solution)/shard_map/psum | solution.py:42
  212.7 1.8 multiply_reduce_fusion.2
  214.5 22.2 %psum.68 = f32[]{:T(128)} all-reduce(f32[]{:T(128)} %multiply_reduce_fusion.2), channel_id=1, replica_groups=mesh['groups'=2,'row'=4,'col'=2,'mpo'=2] {'row','col'}, use_global_device_ids=true, to_apply=%region_11.12 | all-reduce | flops 1 | bytes 8 | tf_op jit(solution)/shard_map/psum | solution.py:44
  236.7 3.1 multiply_reduce_fusion.1
  239.8 17.9 %psum.69 = f32[]{:T(128)} all-reduce(f32[]{:T(128)} %get-tuple-element.2), channel_id=1, replica_groups=mesh['groups'=2,'row'=4,'col'=2,'mpo'=2] {'row','col'}, use_global_device_ids=true, to_apply=%region_13.14 | all-reduce | flops 1 | bytes 8 | tf_op jit(solution)/shard_map/psum | solution.py:48
  258.3 1.0 fusion.37
  259.4 17.1 %all_gather.17 = bf16[12,256,128]{2,1,0:T(8,128)(2,1)} all-gather(bf16[3,256,128]{2,1,0:T(8,128)(2,1)S(1)} %bitcast.53), channel_id=1, replica_groups=mesh['groups'=2,'row'=4,'col'=2,'mpo'=2] {'row'}, dimensions={0}, use_global_device_ids=true | all-gather | bytes 983040 | tf_op jit(solution)/shard_map/all_gather | solution.py:25
  276.5 3.0 gather_fusion.3
  279.5 4.0 %fusion.31 = f32[3,256,256,1]{2,1,3,0:T(8,128)} fusion(bf16[3,7,256,128]{3,2,1,0:T(8,128)(2,1)} %bitcast.46, bf16[7,3,256,256]{3,2,1,0:T(8,128)(2,1)S(1)} %bitcast.43, bf16[7,3,256,128]{3,2,1,0:T(8,128)(2,1)} %bitcast.58), kind=kOutput, calls=%fused_computation.18 | convolution fusion | flops 705331200 | bytes 6291456 | tf_op jit(solution)/shard_map/pkac,kpdc->pad/dot_general | solution.py:39
  283.5 0.0 reduce-scatter.8.cloned.1.call-update
  283.5 0.0 all-reduce.9.cloned.1.call-start
  283.6 16.5 %reduce-scatter.8.cloned.1.call-done = f32[768,128]{1,0:T(8,128)} async-done(((f32[768,256]{1,0:T(8,128)}), f32[768,128]{1,0:T(8,128)}) %reduce-scatter.8.cloned.1.call-update) | async-done | bytes 393232 | tf_op jit(solution)/shard_map/reduce_scatter | solution.py:41
  300.1 20.8 %all-reduce.9.cloned.1.call-done = f32[768,128]{1,0:T(8,128)} async-done(((f32[768,128]{1,0:T(8,128)}), f32[768,128]{1,0:T(8,128)}) %all-reduce.9.cloned.1.call-update) | async-done | bytes 393232 | tf_op jit(solution)/shard_map/psum | solution.py:42
  320.9 1.8 multiply_reduce_fusion
  322.7 22.3 %psum.71 = f32[]{:T(128)} all-reduce(f32[]{:T(128)} %multiply_reduce_fusion), channel_id=1, replica_groups=mesh['groups'=2,'row'=4,'col'=2,'mpo'=2] {'row','col'}, use_global_device_ids=true, to_apply=%region_17.18 | all-reduce | flops 1 | bytes 8 | tf_op jit(solution)/shard_map/psum | solution.py:44
  345.0 2.4 stack.23
  347.4 2.5 multiply_subtract_fusion
  (17 shorter events, 0.1 us)
Async XLA Ops:
  7.2 57.1 %copy-start = (bf16[7,768,256]{2,1,0:T(8,128)(2,1)S(1)}, bf16[7,768,256]{2,1,0:T(8,128)(2,1)}, u32[]{:S(2)}) copy-start(bf16[7,768,256]{2,1,0:T(8,128)(2,1)} %param.7) | copy-start | bytes 8257540
  7.2 14.7 %copy-start.3 = (s32[3,7]{1,0:T(4,128)S(1)}, s32[3,7]{1,0:T(4,128)}, u32[]{:S(2)}) copy-start(s32[3,7]{1,0:T(4,128)} %param.10) | copy-start | bytes 256
  7.2 14.7 %copy-start.4 = (s32[3]{0:T(128)S(1)}, s32[3]{0:T(128)}, u32[]{:S(2)}) copy-start(s32[3]{0:T(128)} %param.11) | copy-start | bytes 40
  7.2 14.8 %copy-start.1 = (f32[768,128]{1,0:T(8,128)S(1)}, f32[768,128]{1,0:T(8,128)}, u32[]{:S(2)}) copy-start(f32[768,128]{1,0:T(8,128)} %param.6) | copy-start | bytes 1179652
  7.2 76.1 %reduce-scatter.4.cloned.1.call-start = ((), (), s32[]{:S(2)}) async-start(), calls=%async_computation.3 | async-start | bytes 1179648 | tf_op jit(solution)/shard_map/reduce_scatter | solution.py:41
  68.2 36.1 %all-reduce.5.cloned.1.call-start = ((), (), s32[]{:S(2)}) async-start(), calls=%async_computation.4 | async-start | bytes 786432 | tf_op jit(solution)/shard_map/psum | solution.py:42
  83.4 108.5 %reduce-scatter.6.cloned.1.call-start = ((), (), s32[]{:S(2)}) async-start(), calls=%async_computation.5 | async-start | bytes 1179648 | tf_op jit(solution)/shard_map/reduce_scatter | solution.py:41
  175.3 37.4 %all-reduce.7.cloned.1.call-start = ((), (), s32[]{:S(2)}) async-start(), calls=%async_computation.6 | async-start | bytes 786432 | tf_op jit(solution)/shard_map/psum | solution.py:42
  191.9 108.2 %reduce-scatter.8.cloned.1.call-start = ((), (), s32[]{:S(2)}) async-start(), calls=%async_computation.7 | async-start | bytes 1179648 | tf_op jit(solution)/shard_map/reduce_scatter | solution.py:41
  283.5 37.5 %copy-start.2 = (f32[768,128]{1,0:T(8,128)S(1)}, f32[768,128]{1,0:T(8,128)}, u32[]{:S(2)}) copy-start(f32[768,128]{1,0:T(8,128)} %get-tuple-element.3) | copy-start | bytes 1179652
  283.5 37.4 %all-reduce.9.cloned.1.call-start = ((), (), s32[]{:S(2)}) async-start(), calls=%async_computation.8 | async-start | bytes 786432 | tf_op jit(solution)/shard_map/psum | solution.py:42
Sparse Core Ops, SparseCore 0:
  68.3 14.9 reduce-scatter.3
  85.8 18.5 all-reduce.4
  175.4 16.4 reduce-scatter.5
  194.2 18.4 all-reduce.6
  283.6 16.4 reduce-scatter.7
  302.4 18.4 all-reduce.8
where the time goes:
time: 358 us; the launch traced here: 357 us
  blocking collectives  187 us (52%)
  waiting for transfers between devices  111 us (31%)
  other arithmetic  18 us (5%)
  between operations  16.3 us (5%)
  local copies, waits for them, and re-layouts  12.5 us (3%)
  matrix products  11.9 us (3%)
    psum x3, blocking collectives, on_device(): alpha = lax.psum(jnp.sum(vector * image), ('row', 'col'))  66.8 us
    psum x3, waiting for transfers between devices, on_device(): image = lax.psum(image, 'mpo')  62.5 us
    all_gather x3, blocking collectives, on_device(): pool = lax.all_gather(blocks, 'row', axis=0, tiled=True)  52.5 us
    reduce_scatter x3, waiting for transfers between devices, on_device(): lax.psum_scatter(partial_sum, 'col', scatter_dimension=1, tiled=True)  48.1 us
    psum x2, blocking collectives, on_device(): resid_sq = lax.psum(jnp.sum(resid * resid), ('row', 'col'))  35.7 us
    psum x1, blocking collectives, on_device(): start_sq = lax.psum(jnp.sum(first * first), ('row', 'col'))  19.3 us
    all_gather x1, blocking collectives, on_device(): table = lax.all_gather(send_list, 'row', axis=0, tiled=True)  12.7 us
    dot_general x3, matrix products, on_device(): jnp.einsum('pkac,kpdc->pad', inner, right, preferred_element_type=jnp.flo...  11.9 us
  transfers between devices with their start and end apart: 6, of which 6 were waited for; matrix products, arithmetic and copies ran while one was open for 0% of the time, Pallas kernels for 0%

commit v1 on v0

v1 whole, which is shorter than its diff:
```python
import functools

import jax
import jax.numpy as jnp
from jax import lax
from jax.experimental import pallas as pl
from jax.experimental.pallas import tpu as pltpu
from jax.sharding import PartitionSpec as P

STEPS = 3
LANES = 128
EPS = 1e-06
MESH = pl.DeviceIdType.MESH


def kernel(
    sizes,
    start_ref,
    left_hbm,
    right_hbm,
    send_ref,
    term_ref,
    len_ref,
    resid_ref,
    coef_ref,
    left,
    right,
    right_t,
    field,
    previous,
    image,
    half,
    pool,
    outgoing,
    inner,
    part,
    from_core,
    to_col,
    from_col,
    sums,
    final,
    load_sem,
    core_send,
    core_recv,
    row_send,
    row_recv,
    pass_send,
    pass_recv,
    part_send,
    part_recv,
    col_send,
    col_recv,
    sum_send,
    sum_recv,
    final_send,
    final_recv,
):
    n_row, n_col, n_mpo = sizes
    k_local, _, width = left_hbm.shape
    sec_dev, rows, columns = field.shape
    cap = send_ref.shape[1] // n_row
    stride = right_t.shape[1] // k_local
    total = n_row * n_col * n_mpo
    row = lax.axis_index("row")
    col = lax.axis_index("col")
    mpo = lax.axis_index("mpo")
    other = lax.rem(mpo + 1, 2)
    mine = (row * n_col + col) * n_mpo + mpo
    my_rows = pl.ds(pl.multiple_of(mpo * rows, rows), rows)
    sibling = {"mpo": other}

    def device(index):
        return {
            "row": index // (n_col * n_mpo),
            "col": lax.rem(index // n_mpo, n_col),
            "mpo": lax.rem(index, n_mpo),
        }

    def peer(step):
        return lax.rem(mine + step, total)

    def remote(src, dst, send, recv, target):
        return pltpu.make_async_remote_copy(
            src_ref=src, dst_ref=dst, send_sem=send, recv_sem=recv,
            device_id=target, device_id_type=MESH,
        )

    loads = []
    for p in range(sec_dev):
        at = pl.multiple_of(p * width + mpo * rows, rows)
        loads.append(pltpu.make_async_copy(start_ref.at[pl.ds(at, rows)], field.at[p], load_sem.at[p]))
    load_right = pltpu.make_async_copy(right_hbm, right, load_sem.at[sec_dev])
    load_left = pltpu.make_async_copy(left_hbm, left, load_sem.at[sec_dev + 1])
    for copy in loads:
        copy.start()
    load_right.start()
    load_left.start()

    barrier = pltpu.get_barrier_semaphore()

    def greet(step, carry):
        pl.semaphore_signal(barrier, inc=1, device_id=device(peer(step)), device_id_type=MESH)
        return carry

    lax.fori_loop(1, total, greet, 0)

    live = []
    for p in range(sec_dev):
        position = lax.broadcasted_iota(jnp.int32, (rows, columns), 0) + mpo * rows
        live.append((position < len_ref[p]).astype(jnp.float32))
    for copy in loads:
        copy.wait()
    for p in range(sec_dev):
        field[p] = field[p] * live[p]
    previous[...] = jnp.zeros_like(previous)
    for j in range(STEPS):
        for c in range(cap):
            pool[j, sec_dev + row * cap + c] = jnp.zeros((width, columns), jnp.bfloat16)
    if stride != columns:
        inner[...] = jnp.zeros_like(inner)
        right_t[...] = jnp.zeros_like(right_t)
    pl.semaphore_wait(barrier, total - 1)

    def exchange(j):
        half[...] = field[...].astype(jnp.bfloat16)
        copies = []
        for step in range(1, n_row):
            target = lax.rem(row + step, n_row)
            for c in range(cap):
                slot = (step - 1) * cap + c
                pick = jnp.maximum(send_ref[0, target * cap + c], 0)
                outgoing[slot] = half[pick]
                place = sec_dev + row * cap + c
                copy = remote(
                    outgoing.at[slot], pool.at[j, place, my_rows],
                    row_send.at[slot], row_recv.at[j, row * cap + c], {"row": target},
                )
                copy.start()
                copies.append(copy)
        pool[j, pl.ds(0, sec_dev), my_rows] = half[...]
        own = remote(
            half, pool.at[j, pl.ds(0, sec_dev), my_rows], core_send, core_recv.at[j], sibling
        )
        own.start()
        return copies + [own]

    def relay(j):
        copies = []
        for step in range(1, n_row):
            source = lax.rem(row + step, n_row)
            for c in range(cap):
                slot = (step - 1) * cap + c
                place = sec_dev + source * cap + c
                block = pool.at[j, place, my_rows]
                remote(
                    outgoing.at[slot], block, row_send.at[slot],
                    row_recv.at[j, source * cap + c], {"row": source},
                ).wait_recv()
                copy = remote(
                    block, block, pass_send.at[slot], pass_recv.at[j, source * cap + c], sibling
                )
                copy.start()
                copies.append(copy)
        their_rows = pl.ds(pl.multiple_of(other * rows, rows), rows)
        remote(
            half, pool.at[j, pl.ds(0, sec_dev), their_rows], core_send, core_recv.at[j], sibling
        ).wait_recv()
        for step in range(1, n_row):
            source = lax.rem(row + step, n_row)
            for c in range(cap):
                slot = (step - 1) * cap + c
                block = pool.at[j, sec_dev + source * cap + c, their_rows]
                remote(
                    block, block, pass_send.at[slot], pass_recv.at[j, source * cap + c], sibling
                ).wait_recv()
        return copies

    def product(j, p):
        for k in range(k_local):
            block = pool[j, term_ref[p, k]]
            value = jnp.dot(
                left[k, p * width:(p + 1) * width, :], block, preferred_element_type=jnp.float32
            )
            inner[p, :, k * stride:k * stride + columns] = value.astype(jnp.bfloat16)
        value = jnp.dot(inner[p], right_t[p], preferred_element_type=jnp.float32)
        for m in range(n_mpo):
            for c in range(n_col):
                part[p, m, c] = value[m * rows:(m + 1) * rows, c * columns:(c + 1) * columns]
        copy = remote(
            part.at[p, other], from_core.at[j, p], part_send.at[p], part_recv.at[j, p], sibling
        )
        copy.start()
        return [copy]

    def add_core(j, p):
        remote(
            part.at[p, other], from_core.at[j, p], part_send.at[p], part_recv.at[j, p], sibling
        ).wait_recv()
        copies = []
        for step in range(1, n_col):
            target = lax.rem(col + step, n_col)
            value = part[p, mpo, target] + from_core[j, p, target]
            to_col[p, step - 1] = value.astype(to_col.dtype)
            copy = remote(
                to_col.at[p, step - 1], from_col.at[j, p, col],
                col_send.at[p, step - 1], col_recv.at[j, p, col], {"col": target},
            )
            copy.start()
            copies.append(copy)
        image[p] = part[p, mpo, col] + from_core[j, p, col]
        return copies

    def add_col(j, p):
        value = image[p]
        for step in range(1, n_col):
            source = lax.rem(col + step, n_col)
            remote(
                to_col.at[p, step - 1], from_col.at[j, p, source],
                col_send.at[p, step - 1], col_recv.at[j, p, source], {"col": source},
            ).wait_recv()
            value = value + from_col[j, p, source].astype(jnp.float32)
        value = value * live[p]
        image[p] = value
        return value

    def fold(value):
        return jnp.sum(value.reshape(rows // 8, 8, columns), axis=0)

    def body(j, carry):
        copies = exchange(j)

        @pl.when(j == 0)
        def _():
            load_right.wait()
            for p in range(sec_dev):
                for k in range(k_local):
                    block = right[k, p * width:(p + 1) * width, :]
                    right_t[p, k * stride:k * stride + columns, :] = block.T
            load_left.wait()

        copies += relay(j)
        copies += product(j, 0)
        for p in range(1, sec_dev):
            copies += product(j, p)
            copies += add_core(j, p - 1)
        copies += add_core(j, sec_dev - 1)
        overlap = jnp.zeros((8, columns), jnp.float32)
        norm = jnp.zeros((8, columns), jnp.float32)
        for p in range(sec_dev):
            u = field[p]
            norm = norm + fold(u * u)
            overlap = overlap + fold(u * add_col(j, p))
        sums[j, mine, 0] = overlap
        sums[j, mine, 1] = norm

        def share(step, carry):
            block = sums.at[j, mine]
            remote(
                block, block, sum_send.at[step], sum_recv.at[j, mine], device(peer(step))
            ).start()
            return carry

        lax.fori_loop(1, total, share, 0)

        def collect(step, carry):
            source = peer(step)
            block = sums.at[j, source]
            remote(
                block, block, sum_send.at[step], sum_recv.at[j, source], device(source)
            ).wait_recv()
            return carry

        lax.fori_loop(1, total, collect, 0)
        added = jnp.sum(sums[j], axis=0)
        overlap = jnp.sum(added[0], keepdims=True)
        norm = jnp.sum(added[1], keepdims=True)
        beta = jnp.sqrt(norm + EPS)
        scale = 1.0 / beta
        alpha = overlap * scale * scale
        for p in range(sec_dev):
            v = field[p] * scale
            field[p] = image[p] * scale - alpha * v - beta * previous[p]
            previous[p] = v
        coef_ref[pl.ds(j, 1)] = jnp.broadcast_to(alpha, (1, LANES))
        coef_ref[pl.ds(STEPS - 1 + j, 1)] = jnp.where(
            j > 0, jnp.broadcast_to(beta, (1, LANES)), jnp.broadcast_to(alpha, (1, LANES))
        )

        for copy in copies:
            copy.wait_send()

        def sent(step, carry):
            block = sums.at[j, mine]
            remote(
                block, block, sum_send.at[step], sum_recv.at[j, mine], device(peer(step))
            ).wait_send()
            return carry

        lax.fori_loop(1, total, sent, 0)
        return carry

    lax.fori_loop(0, STEPS, body, 0)

    copy = remote(field, final, final_send, final_recv, sibling)
    copy.start()
    for p in range(sec_dev):
        at = pl.multiple_of(p * width + mpo * rows, rows)
        resid_ref[pl.ds(at, rows)] = field[p]
    copy.wait_recv()
    for p in range(sec_dev):
        at = pl.multiple_of(p * width + other * rows, rows)
        resid_ref[pl.ds(at, rows)] = final[p]
    copy.wait_send()


def on_device(sizes, start, left_env, right_env, send_list, term_source, sector_len):
    n_row, n_col, n_mpo = sizes
    sec_dev = sector_len.shape[0]
    k_local, height, width = left_env.shape
    columns = start.shape[1]
    rows = width // n_mpo
    stride = max(columns, LANES)
    total = n_row * n_col * n_mpo
    slots = send_list.shape[1]
    cap = slots // n_row
    away = max((n_row - 1) * cap, 1)
    bf, f32 = jnp.bfloat16, jnp.float32
    dma = pltpu.SemaphoreType.DMA
    hbm = pl.BlockSpec(memory_space=pl.ANY)
    smem = pl.BlockSpec(memory_space=pltpu.SMEM)
    vmem = pl.BlockSpec(memory_space=pltpu.VMEM)
    send = jnp.bfloat16
    resid, coef = pl.pallas_call(
        functools.partial(kernel, sizes),
        out_shape=(
            jax.ShapeDtypeStruct((height, columns), f32),
            jax.ShapeDtypeStruct((8, LANES), f32),
        ),
        in_specs=[hbm, hbm, hbm, smem, smem, smem],
        out_specs=(vmem, vmem),
        scratch_shapes=[
            pltpu.VMEM((k_local, height, width), bf),
            pltpu.VMEM((k_local, height, columns), bf),
            pltpu.VMEM((sec_dev, k_local * stride, width), bf),
            pltpu.VMEM((sec_dev, rows, columns), f32),
            pltpu.VMEM((sec_dev, rows, columns), f32),
            pltpu.VMEM((sec_dev, rows, columns), f32),
            pltpu.VMEM((sec_dev, rows, columns), bf),
            pltpu.VMEM((STEPS, sec_dev + slots, width, columns), bf),
            pltpu.VMEM((away, rows, columns), bf),
            pltpu.VMEM((sec_dev, width, k_local * stride), bf),
            pltpu.VMEM((sec_dev, n_mpo, n_col, rows, columns), f32),
            pltpu.VMEM((STEPS, sec_dev, n_col, rows, columns), f32),
            pltpu.VMEM((sec_dev, n_col, rows, columns), send),
            pltpu.VMEM((STEPS, sec_dev, n_col, rows, columns), send),
            pltpu.VMEM((STEPS, total, 2, 8, columns), f32),
            pltpu.VMEM((sec_dev, rows, columns), f32),
            dma((sec_dev + 2,)),
            dma,
            dma((STEPS,)),
            dma((away,)),
            dma((STEPS, slots)),
            dma((away,)),
            dma((STEPS, slots)),
            dma((sec_dev,)),
            dma((STEPS, sec_dev)),
            dma((sec_dev, n_col)),
            dma((STEPS, sec_dev, n_col)),
            dma((total,)),
            dma((STEPS, total)),
            dma,
            dma,
        ],
        compiler_params=pltpu.CompilerParams(
            collective_id=0, has_side_effects=True, vmem_limit_bytes=44 * 1024 * 1024
        ),
    )(start, left_env, right_env, send_list, term_source, sector_len)
    return resid, coef[:2 * STEPS - 1, 0]


def solution(mesh):
    placed = (
        P(("groups", "row"), "col"),
        P("mpo", ("groups", "row"), None),
        P("mpo", ("groups", "row"), "col"),
        P(("groups", "row"), None),
        P(("groups", "row"), "mpo"),
        P(("groups", "row")),
    )
    sizes = (mesh.shape["row"], mesh.shape["col"], mesh.shape["mpo"])
    return jax.shard_map(
        functools.partial(on_device, sizes),
        mesh=mesh,
        in_specs=placed,
        out_specs=(P(("groups", "row"), "col"), P("groups")),
        check_vma=False,
    )
```

time: 358 us -> 69.8 us (0.19)
  blocking collectives: 187 us -> 0 us
  waiting for transfers between devices: 111 us -> 0 us
  Pallas kernels: 0 us -> 61.5 us
  other arithmetic: 18 us -> 0 us
  between operations: 16.3 us -> 0.65 us
  matrix products: 11.9 us -> 0 us
  local copies, waits for them, and re-layouts: 12.5 us -> 7.47 us
    psum x6 -> x0, blocking collectives: 122 us -> none  [the longest x3 66.8 us: on_device(): alpha = lax.psum(jnp.sum(vector * image), ('row', 'col'))]
    all_gather x4 -> x0, blocking collectives: 65.2 us -> none  [the longest x3 52.5 us: on_device(): pool = lax.all_gather(blocks, 'row', axis=0, tiled=True)]
    psum x3 -> x0, waiting for transfers between devices: 62.5 us -> none  [on_device(): image = lax.psum(image, 'mpo')]
    pallas_call x0 -> x1, Pallas kernels: none -> 61.5 us  [on_device(): pl.pallas_call(functools.partial(kernel, sizes), out_shape=(jax.ShapeDtyp...]
    reduce_scatter x3 -> x0, waiting for transfers between devices: 48.1 us -> none  [on_device(): lax.psum_scatter(partial_sum, 'col', scatter_dimension=1, tiled=True)]
    dot_general x3 -> x0, matrix products: 11.9 us -> none  [on_device(): jnp.einsum('pkac,kpdc->pad', inner, right, preferred_element_type=jnp.flo...]
    reduce_sum x6 -> x0, other arithmetic: 11.6 us -> none  [the longest x2 5.47 us: on_device(): resid_sq = lax.psum(jnp.sum(resid * resid), ('row', 'col'))]
    gather x4 -> x0, local copies, waits for them, and re-layouts: 9.86 us -> none  [the longest x3 9.02 us: on_device(): sources = pool[lookup]]
  transfers between devices with their start and end apart: 6 -> 0, of which waited for: 6 -> 0; matrix products, arithmetic and copies ran while one was open for 0% -> 0% of each run, Pallas kernels for 0% -> 0%
where the time goes in v1:
time: 69.8 us; the launch traced here: 69.6 us
  Pallas kernels  61.5 us (88%)
  local copies, waits for them, and re-layouts  7.47 us (11%)
    pallas_call x1, Pallas kernels, on_device(): pl.pallas_call(functools.partial(kernel, sizes), out_shape=(jax.ShapeDtyp...  61.5 us
    unnamed x13, local copies, waits for them, and re-layouts  6.84 us

profile of v1, /device:TPU:0, one launch (start us, length us, event | category | flops | bytes accessed | tf_op | source)
XLA Modules:
  0.0 69.6 jit_solution(10593637041629664170)
XLA Ops:
  0.6 0.0 copy-start
  0.6 1.8 %copy-done = bf16[7,768,256]{2,1,0:T(8,128)(2,1)S(1)} copy-done((bf16[7,768,256]{2,1,0:T(8,128)(2,1)S(1)}, bf16[7,768,256]{2,1,0:T(8,128)(2,1)}, u32[]{:S(2)}) %copy-start) | copy-done | bytes 2752536
  2.4 0.0 copy-start.1
  2.4 1.3 %copy-done.1 = bf16[7,768,128]{2,1,0:T(8,128)(2,1)S(1)} copy-done((bf16[7,768,128]{2,1,0:T(8,128)(2,1)S(1)}, bf16[7,768,128]{2,1,0:T(8,128)(2,1)}, u32[]{:S(2)}) %copy-start.1) | copy-done | bytes 1376280
  3.7 0.0 copy-start.2
  3.8 1.0 %copy-done.2 = f32[768,128]{1,0:T(8,128)S(1)} copy-done((f32[768,128]{1,0:T(8,128)S(1)}, f32[768,128]{1,0:T(8,128)}, u32[]{:S(2)}) %copy-start.2) | copy-done | bytes 393240
  4.7 0.0 copy-start.3
  4.7 0.7 copy-done.3
  5.4 0.0 copy-start.4
  5.4 0.7 copy-done.4
  6.1 0.0 copy-start.5
  6.1 0.7 copy-done.5
  6.7 61.5 %shard_map.77 = (f32[768,128]{1,0:T(8,128)S(1)}, f32[8,128]{1,0:T(8,128)S(1)}) custom-call(f32[768,128]{1,0:T(8,128)S(1)} %copy-done.2, bf16[7,768,256]{2,1,0:T(8,128)(2,1)S(1)} %copy-done, bf16[7,768,128]{2,1,0:T(8,128)(2,1)S(1)} %copy-done.1, s32[1,4]{1,0:T(1,128)S(1)} %copy-done.4, s32[3,7]{1,0:T(4,128)S(1)} %copy-done.3, s32[3]{0:T(128)S(1)} %copy-done.5), custom_call_target="tpu_custom_call" | custom-call | tf_op jit(solution)/shard_map/pallas_call | solution.py:333
  68.2 0.6 slice_reduce_fusion
  68.8 0.7 %copy.9 = f32[768,128]{1,0:T(8,128)} copy(f32[768,128]{1,0:T(8,128)S(1)} %get-tuple-element.8) | data formatting | bytes 786432
Async XLA Ops:
  0.6 1.8 %copy-start = (bf16[7,768,256]{2,1,0:T(8,128)(2,1)S(1)}, bf16[7,768,256]{2,1,0:T(8,128)(2,1)}, u32[]{:S(2)}) copy-start(bf16[7,768,256]{2,1,0:T(8,128)(2,1)} %left_hbm.1) | copy-start | bytes 8257540
  2.4 1.3 %copy-start.1 = (bf16[7,768,128]{2,1,0:T(8,128)(2,1)S(1)}, bf16[7,768,128]{2,1,0:T(8,128)(2,1)}, u32[]{:S(2)}) copy-start(bf16[7,768,128]{2,1,0:T(8,128)(2,1)} %right_hbm.1) | copy-start | bytes 4128772
  3.7 1.0 %copy-start.2 = (f32[768,128]{1,0:T(8,128)S(1)}, f32[768,128]{1,0:T(8,128)}, u32[]{:S(2)}) copy-start(f32[768,128]{1,0:T(8,128)} %start_ref.1) | copy-start | bytes 1179652
  4.7 0.7 copy-start.3
  5.4 0.7 copy-start.4
  6.1 0.7 copy-start.5

commit v2 on v1

--- a/solution.py
+++ b/solution.py
@@ -37,7 +37,8 @@
     from_core,
     to_col,
     from_col,
-    sums,
+    team,
+    line,
     final,
     load_sem,
     core_send,
@@ -50,8 +51,10 @@
     part_recv,
     col_send,
     col_recv,
-    sum_send,
-    sum_recv,
+    team_send,
+    team_recv,
+    line_send,
+    line_recv,
     final_send,
     final_recv,
 ):
@@ -60,24 +63,23 @@
     sec_dev, rows, columns = field.shape
     cap = send_ref.shape[1] // n_row
     stride = right_t.shape[1] // k_local
-    total = n_row * n_col * n_mpo
+    members = n_col * n_mpo
     row = lax.axis_index("row")
     col = lax.axis_index("col")
     mpo = lax.axis_index("mpo")
     other = lax.rem(mpo + 1, 2)
-    mine = (row * n_col + col) * n_mpo + mpo
+    mine = col * n_mpo + mpo
     my_rows = pl.ds(pl.multiple_of(mpo * rows, rows), rows)
     sibling = {"mpo": other}
 
-    def device(index):
-        return {
-            "row": index // (n_col * n_mpo),
-            "col": lax.rem(index // n_mpo, n_col),
-            "mpo": lax.rem(index, n_mpo),
-        }
-
-    def peer(step):
-        return lax.rem(mine + step, total)
+    team_peers = []
+    for step in range(1, members):
+        index = lax.rem(mine + step, members)
+        team_peers.append((index, {"col": index // n_mpo, "mpo": lax.rem(index, n_mpo)}))
+    line_peers = []
+    for step in range(1, n_row):
+        index = lax.rem(row + step, n_row)
+        line_peers.append((index, {"row": index}))
 
     def remote(src, dst, send, recv, target):
         return pltpu.make_async_remote_copy(
@@ -98,11 +100,8 @@
 
     barrier = pltpu.get_barrier_semaphore()
 
-    def greet(step, carry):
-        pl.semaphore_signal(barrier, inc=1, device_id=device(peer(step)), device_id_type=MESH)
-        return carry
-
-    lax.fori_loop(1, total, greet, 0)
+    for _, target in team_peers + line_peers:
+        pl.semaphore_signal(barrier, inc=1, device_id=target, device_id_type=MESH)
 
     live = []
     for p in range(sec_dev):
@@ -119,7 +118,7 @@
     if stride != columns:
         inner[...] = jnp.zeros_like(inner)
         right_t[...] = jnp.zeros_like(right_t)
-    pl.semaphore_wait(barrier, total - 1)
+    pl.semaphore_wait(barrier, len(team_peers) + len(line_peers))
 
     def exchange(j):
         half[...] = field[...].astype(jnp.bfloat16)
@@ -226,8 +225,23 @@
     def fold(value):
         return jnp.sum(value.reshape(rows // 8, 8, columns), axis=0)
 
+    def gather(slots, own, peers, send, recv):
+        block = slots.at[own]
+        copies = []
+        for step, (_, target) in enumerate(peers):
+            copy = remote(block, block, send.at[step], recv.at[own], target)
+            copy.start()
+            copies.append(copy)
+        for step, (index, target) in enumerate(peers):
+            theirs = slots.at[index]
+            remote(theirs, theirs, send.at[step], recv.at[index], target).wait_recv()
+        return copies
+
     def body(j, carry):
         copies = exchange(j)
+        norm = jnp.zeros((8, columns), jnp.float32)
+        for p in range(sec_dev):
+            norm = norm + fold(field[p] * field[p])
 
         @pl.when(j == 0)
         def _():
@@ -245,35 +259,17 @@
             copies += add_core(j, p - 1)
         copies += add_core(j, sec_dev - 1)
         overlap = jnp.zeros((8, columns), jnp.float32)
-        norm = jnp.zeros((8, columns), jnp.float32)
         for p in range(sec_dev):
-            u = field[p]
-            norm = norm + fold(u * u)
-            overlap = overlap + fold(u * add_col(j, p))
-        sums[j, mine, 0] = overlap
-        sums[j, mine, 1] = norm
-
-        def share(step, carry):
-            block = sums.at[j, mine]
-            remote(
-                block, block, sum_send.at[step], sum_recv.at[j, mine], device(peer(step))
-            ).start()
-            return carry
-
-        lax.fori_loop(1, total, share, 0)
-
-        def collect(step, carry):
-            source = peer(step)
-            block = sums.at[j, source]
-            remote(
-                block, block, sum_send.at[step], sum_recv.at[j, source], device(source)
-            ).wait_recv()
-            return carry
-
-        lax.fori_loop(1, total, collect, 0)
-        added = jnp.sum(sums[j], axis=0)
-        overlap = jnp.sum(added[0], keepdims=True)
-        norm = jnp.sum(added[1], keepdims=True)
+            overlap = overlap + fold(field[p] * add_col(j, p))
+        team[j, mine] = jnp.concatenate(
+            [jnp.sum(overlap, axis=0, keepdims=True), jnp.sum(norm, axis=0, keepdims=True)], axis=0
+        )
+        copies += gather(team.at[j], mine, team_peers, team_send, team_recv.at[j])
+        line[j, row] = jnp.sum(team[j], axis=0)
+        copies += gather(line.at[j], row, line_peers, line_send, line_recv.at[j])
+        added = jnp.sum(line[j], axis=0)
+        overlap = jnp.sum(added[0:1], keepdims=True)
+        norm = jnp.sum(added[1:2], keepdims=True)
         beta = jnp.sqrt(norm + EPS)
         scale = 1.0 / beta
         alpha = overlap * scale * scale
@@ -289,14 +285,6 @@
         for copy in copies:
             copy.wait_send()
 
-        def sent(step, carry):
-            block = sums.at[j, mine]
-            remote(
-                block, block, sum_send.at[step], sum_recv.at[j, mine], device(peer(step))
-            ).wait_send()
-            return carry
-
-        lax.fori_loop(1, total, sent, 0)
         return carry
 
     lax.fori_loop(0, STEPS, body, 0)
@@ -320,7 +308,7 @@
     columns = start.shape[1]
     rows = width // n_mpo
     stride = max(columns, LANES)
-    total = n_row * n_col * n_mpo
+    members = n_col * n_mpo
     slots = send_list.shape[1]
     cap = slots // n_row
     away = max((n_row - 1) * cap, 1)
@@ -353,7 +341,8 @@
             pltpu.VMEM((STEPS, sec_dev, n_col, rows, columns), f32),
             pltpu.VMEM((sec_dev, n_col, rows, columns), send),
             pltpu.VMEM((STEPS, sec_dev, n_col, rows, columns), send),
-            pltpu.VMEM((STEPS, total, 2, 8, columns), f32),
+            pltpu.VMEM((STEPS, members, 2, columns), f32),
+            pltpu.VMEM((STEPS, n_row, 2, columns), f32),
             pltpu.VMEM((sec_dev, rows, columns), f32),
             dma((sec_dev + 2,)),
             dma,
@@ -366,13 +355,15 @@
             dma((STEPS, sec_dev)),
             dma((sec_dev, n_col)),
             dma((STEPS, sec_dev, n_col)),
-            dma((total,)),
-            dma((STEPS, total)),
+            dma((members,)),
+            dma((STEPS, members)),
+            dma((n_row,)),
+            dma((STEPS, n_row)),
             dma,
             dma,
         ],
         compiler_params=pltpu.CompilerParams(
-            collective_id=0, has_side_effects=True, vmem_limit_bytes=44 * 1024 * 1024
+            collective_id=0, has_side_effects=True, vmem_limit_bytes=56 * 1024 * 1024
         ),
     )(start, left_env, right_env, send_list, term_source, sector_len)
     return resid, coef[:2 * STEPS - 1, 0]

time: 69.8 us -> 67.6 us (0.968)
  local copies, waits for them, and re-layouts: 7.47 us -> 3.07 us
  Pallas kernels: 61.5 us -> 63.7 us
    unnamed x13 -> x1, local copies, waits for them, and re-layouts: 6.84 us -> 1.77 us
    pallas_call x1, Pallas kernels: 61.5 us -> 63.7 us  [on_device(): pl.pallas_call(functools.partial(kernel, sizes), out_shape=(jax.ShapeDtyp...]
where the time goes in v2:
time: 67.6 us; the launch traced here: 67.4 us
  Pallas kernels  63.7 us (94%)
  local copies, waits for them, and re-layouts  3.07 us (5%)
    pallas_call x1, Pallas kernels, on_device(): pl.pallas_call(functools.partial(kernel, sizes), out_shape=(jax.ShapeDtyp...  63.7 us
    unnamed x1, local copies, waits for them, and re-layouts  1.77 us

profile of v2, /device:TPU:0, one launch (start us, length us, event | category | flops | bytes accessed | tf_op | source)
XLA Modules:
  0.0 67.4 jit_solution(17065780427764848259)
XLA Ops:
  0.6 63.7 %shard_map.77 = (f32[768,128]{1,0:T(8,128)}, f32[8,128]{1,0:T(8,128)}) custom-call(f32[768,128]{1,0:T(8,128)} %start_ref.1, bf16[7,768,256]{2,1,0:T(8,128)(2,1)} %left_hbm.1, bf16[7,768,128]{2,1,0:T(8,128)(2,1)} %right_hbm.1, s32[1,4]{1,0:T(1,128)} %send_ref.1, s32[3,7]{1,0:T(4,128)} %term_ref.1, s32[3]{0:T(128)} %len_ref.1), custom_call_target="tpu_custom_call" | custom-call | tf_op jit(solution)/shard_map/pallas_call | solution.py:321
  64.3 1.3 %slice_reduce_fusion = f32[5]{0:T(128)} fusion(f32[8,128]{1,0:T(8,128)} %get-tuple-element.5), kind=kLoop, calls=%fused_computation | loop fusion | bytes 40 | tf_op jit(solution)/shard_map/slice | solution.py:369
  65.6 1.8 %copy.9 = f32[768,128]{1,0:T(8,128)} copy(f32[768,128]{1,0:T(8,128)} %get-tuple-element.8) | data formatting | bytes 786432

commit v3 on v2

--- a/solution.py
+++ b/solution.py
@@ -10,6 +10,7 @@
 STEPS = 3
 LANES = 128
 EPS = 1e-06
+FLAT = 16
 MESH = pl.DeviceIdType.MESH
 
 
@@ -72,14 +73,27 @@
     my_rows = pl.ds(pl.multiple_of(mpo * rows, rows), rows)
     sibling = {"mpo": other}
 
+    flat = team.shape[1] == n_row * members
     team_peers = []
-    for step in range(1, members):
-        index = lax.rem(mine + step, members)
-        team_peers.append((index, {"col": index // n_mpo, "mpo": lax.rem(index, n_mpo)}))
+    for step in range(1, team.shape[1]):
+        if flat:
+            index = lax.rem(row * members + mine + step, n_row * members)
+            target = {
+                "row": index // members,
+                "col": lax.rem(index // n_mpo, n_col),
+                "mpo": lax.rem(index, n_mpo),
+            }
+        else:
+            index = lax.rem(mine + step, members)
+            target = {"col": index // n_mpo, "mpo": lax.rem(index, n_mpo)}
+        team_peers.append((index, target))
     line_peers = []
     for step in range(1, n_row):
         index = lax.rem(row + step, n_row)
         line_peers.append((index, {"row": index}))
+    if flat:
+        mine = row * members + mine
+    greeted = team_peers if flat else team_peers + line_peers
 
     def remote(src, dst, send, recv, target):
         return pltpu.make_async_remote_copy(
@@ -100,7 +114,7 @@
 
     barrier = pltpu.get_barrier_semaphore()
 
-    for _, target in team_peers + line_peers:
+    for _, target in greeted:
         pl.semaphore_signal(barrier, inc=1, device_id=target, device_id_type=MESH)
 
     live = []
@@ -118,33 +132,29 @@
     if stride != columns:
         inner[...] = jnp.zeros_like(inner)
         right_t[...] = jnp.zeros_like(right_t)
-    pl.semaphore_wait(barrier, len(team_peers) + len(line_peers))
+    pl.semaphore_wait(barrier, len(greeted))
 
     def exchange(j):
-        half[...] = field[...].astype(jnp.bfloat16)
-        copies = []
+        half[j] = field[...].astype(jnp.bfloat16)
         for step in range(1, n_row):
             target = lax.rem(row + step, n_row)
             for c in range(cap):
                 slot = (step - 1) * cap + c
                 pick = jnp.maximum(send_ref[0, target * cap + c], 0)
-                outgoing[slot] = half[pick]
+                outgoing[j, slot] = half[j, pick]
                 place = sec_dev + row * cap + c
                 copy = remote(
-                    outgoing.at[slot], pool.at[j, place, my_rows],
-                    row_send.at[slot], row_recv.at[j, row * cap + c], {"row": target},
+                    outgoing.at[j, slot], pool.at[j, place, my_rows],
+                    row_send.at[j, slot], row_recv.at[j, row * cap + c], {"row": target},
                 )
                 copy.start()
-                copies.append(copy)
-        pool[j, pl.ds(0, sec_dev), my_rows] = half[...]
+        pool[j, pl.ds(0, sec_dev), my_rows] = half[j]
         own = remote(
-            half, pool.at[j, pl.ds(0, sec_dev), my_rows], core_send, core_recv.at[j], sibling
+            half.at[j], pool.at[j, pl.ds(0, sec_dev), my_rows], core_send.at[j], core_recv.at[j], sibling
         )
         own.start()
-        return copies + [own]
 
     def relay(j):
-        copies = []
         for step in range(1, n_row):
             source = lax.rem(row + step, n_row)
             for c in range(cap):
@@ -152,17 +162,16 @@
                 place = sec_dev + source * cap + c
                 block = pool.at[j, place, my_rows]
                 remote(
-                    outgoing.at[slot], block, row_send.at[slot],
+                    outgoing.at[j, slot], block, row_send.at[j, slot],
                     row_recv.at[j, source * cap + c], {"row": source},
                 ).wait_recv()
                 copy = remote(
-                    block, block, pass_send.at[slot], pass_recv.at[j, source * cap + c], sibling
+                    block, block, pass_send.at[j, slot], pass_recv.at[j, source * cap + c], sibling
                 )
                 copy.start()
-                copies.append(copy)
         their_rows = pl.ds(pl.multiple_of(other * rows, rows), rows)
         remote(
-            half, pool.at[j, pl.ds(0, sec_dev), their_rows], core_send, core_recv.at[j], sibling
+            half.at[j], pool.at[j, pl.ds(0, sec_dev), their_rows], core_send.at[j], core_recv.at[j], sibling
         ).wait_recv()
         for step in range(1, n_row):
             source = lax.rem(row + step, n_row)
@@ -170,9 +179,8 @@
                 slot = (step - 1) * cap + c
                 block = pool.at[j, sec_dev + source * cap + c, their_rows]
                 remote(
-                    block, block, pass_send.at[slot], pass_recv.at[j, source * cap + c], sibling
+                    block, block, pass_send.at[j, slot], pass_recv.at[j, source * cap + c], sibling
                 ).wait_recv()
-        return copies
 
     def product(j, p):
         for k in range(k_local):
@@ -184,38 +192,34 @@
         value = jnp.dot(inner[p], right_t[p], preferred_element_type=jnp.float32)
         for m in range(n_mpo):
             for c in range(n_col):
-                part[p, m, c] = value[m * rows:(m + 1) * rows, c * columns:(c + 1) * columns]
+                part[j, p, m, c] = value[m * rows:(m + 1) * rows, c * columns:(c + 1) * columns]
         copy = remote(
-            part.at[p, other], from_core.at[j, p], part_send.at[p], part_recv.at[j, p], sibling
+            part.at[j, p, other], from_core.at[j, p], part_send.at[j, p], part_recv.at[j, p], sibling
         )
         copy.start()
-        return [copy]
 
     def add_core(j, p):
         remote(
-            part.at[p, other], from_core.at[j, p], part_send.at[p], part_recv.at[j, p], sibling
+            part.at[j, p, other], from_core.at[j, p], part_send.at[j, p], part_recv.at[j, p], sibling
         ).wait_recv()
-        copies = []
         for step in range(1, n_col):
             target = lax.rem(col + step, n_col)
-            value = part[p, mpo, target] + from_core[j, p, target]
-            to_col[p, step - 1] = value.astype(to_col.dtype)
+            value = part[j, p, mpo, target] + from_core[j, p, target]
+            to_col[j, p, step - 1] = value.astype(to_col.dtype)
             copy = remote(
-                to_col.at[p, step - 1], from_col.at[j, p, col],
-                col_send.at[p, step - 1], col_recv.at[j, p, col], {"col": target},
+                to_col.at[j, p, step - 1], from_col.at[j, p, col],
+                col_send.at[j, p, step - 1], col_recv.at[j, p, col], {"col": target},
             )
             copy.start()
-            copies.append(copy)
-        image[p] = part[p, mpo, col] + from_core[j, p, col]
-        return copies
+        image[p] = part[j, p, mpo, col] + from_core[j, p, col]
 
     def add_col(j, p):
         value = image[p]
         for step in range(1, n_col):
             source = lax.rem(col + step, n_col)
             remote(
-                to_col.at[p, step - 1], from_col.at[j, p, source],
-                col_send.at[p, step - 1], col_recv.at[j, p, source], {"col": source},
+                to_col.at[j, p, step - 1], from_col.at[j, p, source],
+                col_send.at[j, p, step - 1], col_recv.at[j, p, source], {"col": source},
             ).wait_recv()
             value = value + from_col[j, p, source].astype(jnp.float32)
         value = value * live[p]
@@ -227,18 +231,15 @@
 
     def gather(slots, own, peers, send, recv):
         block = slots.at[own]
-        copies = []
         for step, (_, target) in enumerate(peers):
             copy = remote(block, block, send.at[step], recv.at[own], target)
             copy.start()
-            copies.append(copy)
         for step, (index, target) in enumerate(peers):
             theirs = slots.at[index]
             remote(theirs, theirs, send.at[step], recv.at[index], target).wait_recv()
-        return copies
 
     def body(j, carry):
-        copies = exchange(j)
+        exchange(j)
         norm = jnp.zeros((8, columns), jnp.float32)
         for p in range(sec_dev):
             norm = norm + fold(field[p] * field[p])
@@ -252,22 +253,24 @@
                     right_t[p, k * stride:k * stride + columns, :] = block.T
             load_left.wait()
 
-        copies += relay(j)
-        copies += product(j, 0)
+        relay(j)
+        product(j, 0)
         for p in range(1, sec_dev):
-            copies += product(j, p)
-            copies += add_core(j, p - 1)
-        copies += add_core(j, sec_dev - 1)
+            product(j, p)
+            add_core(j, p - 1)
+        add_core(j, sec_dev - 1)
         overlap = jnp.zeros((8, columns), jnp.float32)
         for p in range(sec_dev):
             overlap = overlap + fold(field[p] * add_col(j, p))
         team[j, mine] = jnp.concatenate(
             [jnp.sum(overlap, axis=0, keepdims=True), jnp.sum(norm, axis=0, keepdims=True)], axis=0
         )
-        copies += gather(team.at[j], mine, team_peers, team_send, team_recv.at[j])
-        line[j, row] = jnp.sum(team[j], axis=0)
-        copies += gather(line.at[j], row, line_peers, line_send, line_recv.at[j])
-        added = jnp.sum(line[j], axis=0)
+        gather(team.at[j], mine, team_peers, team_send.at[j], team_recv.at[j])
+        added = jnp.sum(team[j], axis=0)
+        if not flat:
+            line[j, row] = added
+            gather(line.at[j], row, line_peers, line_send.at[j], line_recv.at[j])
+            added = jnp.sum(line[j], axis=0)
         overlap = jnp.sum(added[0:1], keepdims=True)
         norm = jnp.sum(added[1:2], keepdims=True)
         beta = jnp.sqrt(norm + EPS)
@@ -282,9 +285,29 @@
             j > 0, jnp.broadcast_to(beta, (1, LANES)), jnp.broadcast_to(alpha, (1, LANES))
         )
 
-        for copy in copies:
-            copy.wait_send()
-
+        return carry
+
+    def drain(j, carry):
+        for slot in range((n_row - 1) * cap):
+            block = outgoing.at[j, slot]
+            remote(block, block, row_send.at[j, slot], row_recv.at[j, 0], sibling).wait_send()
+            remote(block, block, pass_send.at[j, slot], row_recv.at[j, 0], sibling).wait_send()
+        remote(half.at[j], half.at[j], core_send.at[j], core_recv.at[j], sibling).wait_send()
+        for p in range(sec_dev):
+            block = part.at[j, p, other]
+            remote(block, block, part_send.at[j, p], part_recv.at[j, p], sibling).wait_send()
+            for step in range(1, n_col):
+                block = to_col.at[j, p, step - 1]
+                remote(
+                    block, block, col_send.at[j, p, step - 1], col_recv.at[j, p, 0], sibling
+                ).wait_send()
+        block = team.at[j, mine]
+        for step in range(len(team_peers)):
+            remote(block, block, team_send.at[j, step], team_recv.at[j, 0], sibling).wait_send()
+        if not flat:
+            block = line.at[j, row]
+            for step in range(len(line_peers)):
+                remote(block, block, line_send.at[j, step], line_recv.at[j, 0], sibling).wait_send()
         return carry
 
     lax.fori_loop(0, STEPS, body, 0)
@@ -299,6 +322,7 @@
         at = pl.multiple_of(p * width + other * rows, rows)
         resid_ref[pl.ds(at, rows)] = final[p]
     copy.wait_send()
+    lax.fori_loop(0, STEPS, drain, 0)
 
 
 def on_device(sizes, start, left_env, right_env, send_list, term_source, sector_len):
@@ -309,6 +333,7 @@
     rows = width // n_mpo
     stride = max(columns, LANES)
     members = n_col * n_mpo
+    team = n_row * members if n_row * members <= FLAT else members
     slots = send_list.shape[1]
     cap = slots // n_row
     away = max((n_row - 1) * cap, 1)
@@ -333,31 +358,31 @@
             pltpu.VMEM((sec_dev, rows, columns), f32),
             pltpu.VMEM((sec_dev, rows, columns), f32),
             pltpu.VMEM((sec_dev, rows, columns), f32),
-            pltpu.VMEM((sec_dev, rows, columns), bf),
+            pltpu.VMEM((STEPS, sec_dev, rows, columns), bf),
             pltpu.VMEM((STEPS, sec_dev + slots, width, columns), bf),
-            pltpu.VMEM((away, rows, columns), bf),
+            pltpu.VMEM((STEPS, away, rows, columns), bf),
             pltpu.VMEM((sec_dev, width, k_local * stride), bf),
-            pltpu.VMEM((sec_dev, n_mpo, n_col, rows, columns), f32),
+            pltpu.VMEM((STEPS, sec_dev, n_mpo, n_col, rows, columns), f32),
             pltpu.VMEM((STEPS, sec_dev, n_col, rows, columns), f32),
-            pltpu.VMEM((sec_dev, n_col, rows, columns), send),
             pltpu.VMEM((STEPS, sec_dev, n_col, rows, columns), send),
-            pltpu.VMEM((STEPS, members, 2, columns), f32),
+            pltpu.VMEM((STEPS, sec_dev, n_col, rows, columns), send),
+            pltpu.VMEM((STEPS, team, 2, columns), f32),
             pltpu.VMEM((STEPS, n_row, 2, columns), f32),
             pltpu.VMEM((sec_dev, rows, columns), f32),
             dma((sec_dev + 2,)),
-            dma,
             dma((STEPS,)),
-            dma((away,)),
+            dma((STEPS,)),
+            dma((STEPS, away)),
             dma((STEPS, slots)),
-            dma((away,)),
+            dma((STEPS, away)),
             dma((STEPS, slots)),
-            dma((sec_dev,)),
             dma((STEPS, sec_dev)),
-            dma((sec_dev, n_col)),
+            dma((STEPS, sec_dev)),
             dma((STEPS, sec_dev, n_col)),
-            dma((members,)),
-            dma((STEPS, members)),
-            dma((n_row,)),
+            dma((STEPS, sec_dev, n_col)),
+            dma((STEPS, team)),
+            dma((STEPS, team)),
+            dma((STEPS, n_row)),
             dma((STEPS, n_row)),
             dma,
             dma,

time: 67.6 us -> 64.8 us (0.959)
  Pallas kernels: 63.7 us -> 60.9 us
    pallas_call x1, Pallas kernels: 63.7 us -> 60.9 us  [on_device(): pl.pallas_call(functools.partial(kernel, sizes), out_shape=(jax.ShapeDtyp...]
where the time goes in v3:
time: 64.8 us; the launch traced here: 64.6 us
  Pallas kernels  60.9 us (94%)
  local copies, waits for them, and re-layouts  3.07 us (5%)
    pallas_call x1, Pallas kernels, on_device(): pl.pallas_call(functools.partial(kernel, sizes), out_shape=(jax.ShapeDtyp...  60.9 us
    unnamed x1, local copies, waits for them, and re-layouts  1.77 us
    slice x1, local copies, waits for them, and re-layouts, on_device(): return (resid, coef[:2 * STEPS - 1, 0])  1.3 us

profile of v3, /device:TPU:0, one launch (start us, length us, event | category | flops | bytes accessed | tf_op | source)
XLA Modules:
  0.0 64.6 jit_solution(6060142280786999849)
XLA Ops:
  0.6 60.9 %shard_map.77 = (f32[768,128]{1,0:T(8,128)}, f32[8,128]{1,0:T(8,128)}) custom-call(f32[768,128]{1,0:T(8,128)} %start_ref.1, bf16[7,768,256]{2,1,0:T(8,128)(2,1)} %left_hbm.1, bf16[7,768,128]{2,1,0:T(8,128)(2,1)} %right_hbm.1, s32[1,4]{1,0:T(1,128)} %send_ref.1, s32[3,7]{1,0:T(4,128)} %term_ref.1, s32[3]{0:T(128)} %len_ref.1), custom_call_target="tpu_custom_call" | custom-call | tf_op jit(solution)/shard_map/pallas_call | solution.py:346
  61.6 1.3 %slice_reduce_fusion = f32[5]{0:T(128)} fusion(f32[8,128]{1,0:T(8,128)} %get-tuple-element.5), kind=kLoop, calls=%fused_computation | loop fusion | bytes 40 | tf_op jit(solution)/shard_map/slice | solution.py:394
  62.9 1.8 %copy.9 = f32[768,128]{1,0:T(8,128)} copy(f32[768,128]{1,0:T(8,128)} %get-tuple-element.8) | data formatting | bytes 786432

commit v4 on v3

--- a/solution.py
+++ b/solution.py
@@ -38,6 +38,7 @@
     from_core,
     to_col,
     from_col,
+    across,
     team,
     line,
     final,
@@ -52,6 +53,8 @@
     part_recv,
     col_send,
     col_recv,
+    across_send,
+    across_recv,
     team_send,
     team_recv,
     line_send,
@@ -153,6 +156,12 @@
             half.at[j], pool.at[j, pl.ds(0, sec_dev), my_rows], core_send.at[j], core_recv.at[j], sibling
         )
         own.start()
+        for step in range(1, n_col):
+            target = lax.rem(col + step, n_col)
+            remote(
+                field, across.at[j, col], across_send.at[j, step], across_recv.at[j, col],
+                {"col": target},
+            ).start()
 
     def relay(j):
         for step in range(1, n_row):
@@ -202,16 +211,29 @@
         remote(
             part.at[j, p, other], from_core.at[j, p], part_send.at[j, p], part_recv.at[j, p], sibling
         ).wait_recv()
+        values = []
         for step in range(1, n_col):
             target = lax.rem(col + step, n_col)
             value = part[j, p, mpo, target] + from_core[j, p, target]
+            values.append(value)
             to_col[j, p, step - 1] = value.astype(to_col.dtype)
             copy = remote(
                 to_col.at[j, p, step - 1], from_col.at[j, p, col],
                 col_send.at[j, p, step - 1], col_recv.at[j, p, col], {"col": target},
             )
             copy.start()
-        image[p] = part[j, p, mpo, col] + from_core[j, p, col]
+        value = part[j, p, mpo, col] + from_core[j, p, col]
+        image[p] = value
+        overlap = fold(field[p] * value)
+        for step in range(1, n_col):
+            source = lax.rem(col + step, n_col)
+            if p == 0:
+                theirs = across.at[j, source]
+                remote(
+                    theirs, theirs, across_send.at[j, step], across_recv.at[j, source], sibling
+                ).wait_recv()
+            overlap = overlap + fold(across[j, source, p] * values[step - 1])
+        return overlap
 
     def add_col(j, p):
         value = image[p]
@@ -222,18 +244,17 @@
                 col_send.at[j, p, step - 1], col_recv.at[j, p, source], {"col": source},
             ).wait_recv()
             value = value + from_col[j, p, source].astype(jnp.float32)
-        value = value * live[p]
-        image[p] = value
-        return value
+        image[p] = value * live[p]
 
     def fold(value):
         return jnp.sum(value.reshape(rows // 8, 8, columns), axis=0)
 
-    def gather(slots, own, peers, send, recv):
+    def spread(slots, own, peers, send, recv):
         block = slots.at[own]
         for step, (_, target) in enumerate(peers):
-            copy = remote(block, block, send.at[step], recv.at[own], target)
-            copy.start()
+            remote(block, block, send.at[step], recv.at[own], target).start()
+
+    def collect(slots, peers, send, recv):
         for step, (index, target) in enumerate(peers):
             theirs = slots.at[index]
             remote(theirs, theirs, send.at[step], recv.at[index], target).wait_recv()
@@ -255,27 +276,33 @@
 
         relay(j)
         product(j, 0)
+        overlap = jnp.zeros((8, columns), jnp.float32)
         for p in range(1, sec_dev):
             product(j, p)
-            add_core(j, p - 1)
-        add_core(j, sec_dev - 1)
-        overlap = jnp.zeros((8, columns), jnp.float32)
-        for p in range(sec_dev):
-            overlap = overlap + fold(field[p] * add_col(j, p))
+            overlap = overlap + add_core(j, p - 1)
+        overlap = overlap + add_core(j, sec_dev - 1)
         team[j, mine] = jnp.concatenate(
             [jnp.sum(overlap, axis=0, keepdims=True), jnp.sum(norm, axis=0, keepdims=True)], axis=0
         )
-        gather(team.at[j], mine, team_peers, team_send.at[j], team_recv.at[j])
+        spread(team.at[j], mine, team_peers, team_send.at[j], team_recv.at[j])
+        for p in range(sec_dev):
+            add_col(j, p)
+        collect(team.at[j], team_peers, team_send.at[j], team_recv.at[j])
         added = jnp.sum(team[j], axis=0)
         if not flat:
             line[j, row] = added
-            gather(line.at[j], row, line_peers, line_send.at[j], line_recv.at[j])
+            spread(line.at[j], row, line_peers, line_send.at[j], line_recv.at[j])
+            collect(line.at[j], line_peers, line_send.at[j], line_recv.at[j])
             added = jnp.sum(line[j], axis=0)
         overlap = jnp.sum(added[0:1], keepdims=True)
         norm = jnp.sum(added[1:2], keepdims=True)
         beta = jnp.sqrt(norm + EPS)
         scale = 1.0 / beta
         alpha = overlap * scale * scale
+        for step in range(1, n_col):
+            remote(
+                field, across.at[j, col], across_send.at[j, step], across_recv.at[j, col], sibling
+            ).wait_send()
         for p in range(sec_dev):
             v = field[p] * scale
             field[p] = image[p] * scale - alpha * v - beta * previous[p]
@@ -366,6 +393,7 @@
             pltpu.VMEM((STEPS, sec_dev, n_col, rows, columns), f32),
             pltpu.VMEM((STEPS, sec_dev, n_col, rows, columns), send),
             pltpu.VMEM((STEPS, sec_dev, n_col, rows, columns), send),
+            pltpu.VMEM((STEPS, n_col, sec_dev, rows, columns), f32),
             pltpu.VMEM((STEPS, team, 2, columns), f32),
             pltpu.VMEM((STEPS, n_row, 2, columns), f32),
             pltpu.VMEM((sec_dev, rows, columns), f32),
@@ -380,6 +408,8 @@
             dma((STEPS, sec_dev)),
             dma((STEPS, sec_dev, n_col)),
             dma((STEPS, sec_dev, n_col)),
+            dma((STEPS, n_col)),
+            dma((STEPS, n_col)),
             dma((STEPS, team)),
             dma((STEPS, team)),
             dma((STEPS, n_row)),

time: 64.8 us -> 55.3 us (0.85)
  Pallas kernels: 60.9 us -> 51.3 us
    pallas_call x1, Pallas kernels: 60.9 us -> 51.3 us  [on_device(): pl.pallas_call(functools.partial(kernel, sizes), out_shape=(jax.ShapeDtyp...]
where the time goes in v4:
time: 55.3 us; the launch traced here: 55.1 us
  Pallas kernels  51.3 us (93%)
  local copies, waits for them, and re-layouts  3.07 us (6%)
  between operations  0.64 us (1%)
    pallas_call x1, Pallas kernels, on_device(): pl.pallas_call(functools.partial(kernel, sizes), out_shape=(jax.ShapeDtyp...  51.3 us
    unnamed x1, local copies, waits for them, and re-layouts  1.77 us
    slice x1, local copies, waits for them, and re-layouts, on_device(): return (resid, coef[:2 * STEPS - 1, 0])  1.3 us

profile of v4, /device:TPU:0, one launch (start us, length us, event | category | flops | bytes accessed | tf_op | source)
XLA Modules:
  0.0 55.1 jit_solution(6857953125839194105)
XLA Ops:
  0.6 51.3 %shard_map.77 = (f32[768,128]{1,0:T(8,128)}, f32[8,128]{1,0:T(8,128)}) custom-call(f32[768,128]{1,0:T(8,128)} %start_ref.1, bf16[7,768,256]{2,1,0:T(8,128)(2,1)} %left_hbm.1, bf16[7,768,128]{2,1,0:T(8,128)(2,1)} %right_hbm.1, s32[1,4]{1,0:T(1,128)} %send_ref.1, s32[3,7]{1,0:T(4,128)} %term_ref.1, s32[3]{0:T(128)} %len_ref.1), custom_call_target="tpu_custom_call" | custom-call | tf_op jit(solution)/shard_map/pallas_call | solution.py:373
  52.0 1.3 %slice_reduce_fusion = f32[5]{0:T(128)} fusion(f32[8,128]{1,0:T(8,128)} %get-tuple-element.5), kind=kLoop, calls=%fused_computation | loop fusion | bytes 40 | tf_op jit(solution)/shard_map/slice | solution.py:424
  53.3 1.8 %copy.9 = f32[768,128]{1,0:T(8,128)} copy(f32[768,128]{1,0:T(8,128)} %get-tuple-element.8) | data formatting | bytes 786432

commit v5 on v4

--- a/solution.py
+++ b/solution.py
@@ -19,9 +19,9 @@
     start_ref,
     left_hbm,
     right_hbm,
-    send_ref,
-    term_ref,
-    len_ref,
+    send_hbm,
+    term_hbm,
+    len_hbm,
     resid_ref,
     coef_ref,
     left,
@@ -42,6 +42,9 @@
     team,
     line,
     final,
+    send_ref,
+    term_ref,
+    len_ref,
     load_sem,
     core_send,
     core_recv,
@@ -77,10 +80,11 @@
     sibling = {"mpo": other}
 
     flat = team.shape[1] == n_row * members
+    turn = 1 - 2 * (row // max((n_row + 1) // 2, 1))
     team_peers = []
     for step in range(1, team.shape[1]):
         if flat:
-            index = lax.rem(row * members + mine + step, n_row * members)
+            index = lax.rem(row * members + mine + n_row * members - turn * step, n_row * members)
             target = {
                 "row": index // members,
                 "col": lax.rem(index // n_mpo, n_col),
@@ -110,6 +114,9 @@
         loads.append(pltpu.make_async_copy(start_ref.at[pl.ds(at, rows)], field.at[p], load_sem.at[p]))
     load_right = pltpu.make_async_copy(right_hbm, right, load_sem.at[sec_dev])
     load_left = pltpu.make_async_copy(left_hbm, left, load_sem.at[sec_dev + 1])
+    small = ((send_hbm, send_ref), (term_hbm, term_ref), (len_hbm, len_ref))
+    for i, (src, dst) in enumerate(small):
+        loads.append(pltpu.make_async_copy(src, dst, load_sem.at[sec_dev + 2 + i]))
     for copy in loads:
         copy.start()
     load_right.start()
@@ -120,12 +127,12 @@
     for _, target in greeted:
         pl.semaphore_signal(barrier, inc=1, device_id=target, device_id_type=MESH)
 
+    for copy in loads:
+        copy.wait()
     live = []
     for p in range(sec_dev):
         position = lax.broadcasted_iota(jnp.int32, (rows, columns), 0) + mpo * rows
         live.append((position < len_ref[p]).astype(jnp.float32))
-    for copy in loads:
-        copy.wait()
     for p in range(sec_dev):
         field[p] = field[p] * live[p]
     previous[...] = jnp.zeros_like(previous)
@@ -140,7 +147,7 @@
     def exchange(j):
         half[j] = field[...].astype(jnp.bfloat16)
         for step in range(1, n_row):
-            target = lax.rem(row + step, n_row)
+            target = lax.rem(row - turn * step + n_row, n_row)
             for c in range(cap):
                 slot = (step - 1) * cap + c
                 pick = jnp.maximum(send_ref[0, target * cap + c], 0)
@@ -165,7 +172,7 @@
 
     def relay(j):
         for step in range(1, n_row):
-            source = lax.rem(row + step, n_row)
+            source = lax.rem(row + turn * step + n_row, n_row)
             for c in range(cap):
                 slot = (step - 1) * cap + c
                 place = sec_dev + source * cap + c
@@ -183,7 +190,7 @@
             half.at[j], pool.at[j, pl.ds(0, sec_dev), their_rows], core_send.at[j], core_recv.at[j], sibling
         ).wait_recv()
         for step in range(1, n_row):
-            source = lax.rem(row + step, n_row)
+            source = lax.rem(row + turn * step + n_row, n_row)
             for c in range(cap):
                 slot = (step - 1) * cap + c
                 block = pool.at[j, sec_dev + source * cap + c, their_rows]
@@ -259,8 +266,35 @@
             theirs = slots.at[index]
             remote(theirs, theirs, send.at[step], recv.at[index], target).wait_recv()
 
+    def drain(j):
+        for slot in range((n_row - 1) * cap):
+            block = outgoing.at[j, slot]
+            remote(block, block, row_send.at[j, slot], row_recv.at[j, 0], sibling).wait_send()
+            remote(block, block, pass_send.at[j, slot], row_recv.at[j, 0], sibling).wait_send()
+        remote(half.at[j], half.at[j], core_send.at[j], core_recv.at[j], sibling).wait_send()
+        for p in range(sec_dev):
+            block = part.at[j, p, other]
+            remote(block, block, part_send.at[j, p], part_recv.at[j, p], sibling).wait_send()
+            for step in range(1, n_col):
+                block = to_col.at[j, p, step - 1]
+                remote(
+                    block, block, col_send.at[j, p, step - 1], col_recv.at[j, p, 0], sibling
+                ).wait_send()
+        block = team.at[j, mine]
+        for step in range(len(team_peers)):
+            remote(block, block, team_send.at[j, step], team_recv.at[j, 0], sibling).wait_send()
+        if not flat:
+            block = line.at[j, row]
+            for step in range(len(line_peers)):
+                remote(block, block, line_send.at[j, step], line_recv.at[j, 0], sibling).wait_send()
+
     def body(j, carry):
         exchange(j)
+
+        @pl.when(j > 0)
+        def _():
+            drain(j - 1)
+
         norm = jnp.zeros((8, columns), jnp.float32)
         for p in range(sec_dev):
             norm = norm + fold(field[p] * field[p])
@@ -314,29 +348,6 @@
 
         return carry
 
-    def drain(j, carry):
-        for slot in range((n_row - 1) * cap):
-            block = outgoing.at[j, slot]
-            remote(block, block, row_send.at[j, slot], row_recv.at[j, 0], sibling).wait_send()
-            remote(block, block, pass_send.at[j, slot], row_recv.at[j, 0], sibling).wait_send()
-        remote(half.at[j], half.at[j], core_send.at[j], core_recv.at[j], sibling).wait_send()
-        for p in range(sec_dev):
-            block = part.at[j, p, other]
-            remote(block, block, part_send.at[j, p], part_recv.at[j, p], sibling).wait_send()
-            for step in range(1, n_col):
-                block = to_col.at[j, p, step - 1]
-                remote(
-                    block, block, col_send.at[j, p, step - 1], col_recv.at[j, p, 0], sibling
-                ).wait_send()
-        block = team.at[j, mine]
-        for step in range(len(team_peers)):
-            remote(block, block, team_send.at[j, step], team_recv.at[j, 0], sibling).wait_send()
-        if not flat:
-            block = line.at[j, row]
-            for step in range(len(line_peers)):
-                remote(block, block, line_send.at[j, step], line_recv.at[j, 0], sibling).wait_send()
-        return carry
-
     lax.fori_loop(0, STEPS, body, 0)
 
     copy = remote(field, final, final_send, final_recv, sibling)
@@ -344,12 +355,12 @@
     for p in range(sec_dev):
         at = pl.multiple_of(p * width + mpo * rows, rows)
         resid_ref[pl.ds(at, rows)] = field[p]
+    drain(STEPS - 1)
     copy.wait_recv()
     for p in range(sec_dev):
         at = pl.multiple_of(p * width + other * rows, rows)
         resid_ref[pl.ds(at, rows)] = final[p]
     copy.wait_send()
-    lax.fori_loop(0, STEPS, drain, 0)
 
 
 def on_device(sizes, start, left_env, right_env, send_list, term_source, sector_len):
@@ -367,7 +378,6 @@
     bf, f32 = jnp.bfloat16, jnp.float32
     dma = pltpu.SemaphoreType.DMA
     hbm = pl.BlockSpec(memory_space=pl.ANY)
-    smem = pl.BlockSpec(memory_space=pltpu.SMEM)
     vmem = pl.BlockSpec(memory_space=pltpu.VMEM)
     send = jnp.bfloat16
     resid, coef = pl.pallas_call(
@@ -376,7 +386,7 @@
             jax.ShapeDtypeStruct((height, columns), f32),
             jax.ShapeDtypeStruct((8, LANES), f32),
         ),
-        in_specs=[hbm, hbm, hbm, smem, smem, smem],
+        in_specs=[hbm] * 6,
         out_specs=(vmem, vmem),
         scratch_shapes=[
             pltpu.VMEM((k_local, height, width), bf),
@@ -397,7 +407,10 @@
             pltpu.VMEM((STEPS, team, 2, columns), f32),
             pltpu.VMEM((STEPS, n_row, 2, columns), f32),
             pltpu.VMEM((sec_dev, rows, columns), f32),
-            dma((sec_dev + 2,)),
+            pltpu.SMEM(send_list.shape, jnp.int32),
+            pltpu.SMEM(term_source.shape, jnp.int32),
+            pltpu.SMEM(sector_len.shape, jnp.int32),
+            dma((sec_dev + 5,)),
             dma((STEPS,)),
             dma((STEPS,)),
             dma((STEPS, away)),

time: 55.3 us -> 52 us (0.940)
  Pallas kernels: 51.3 us -> 48.1 us
    pallas_call x1, Pallas kernels: 51.3 us -> 48.1 us  [on_device(): pl.pallas_call(functools.partial(kernel, sizes), out_shape=(jax.ShapeDtyp...]
where the time goes in v5:
time: 52 us; the launch traced here: 51.8 us
  Pallas kernels  48.1 us (92%)
  local copies, waits for them, and re-layouts  3.07 us (6%)
  between operations  0.64 us (1%)
    pallas_call x1, Pallas kernels, on_device(): pl.pallas_call(functools.partial(kernel, sizes), out_shape=(jax.ShapeDtyp...  48.1 us
    unnamed x1, local copies, waits for them, and re-layouts  1.77 us
    slice x1, local copies, waits for them, and re-layouts, on_device(): return (resid, coef[:2 * STEPS - 1, 0])  1.3 us

profile of v5, /device:TPU:0, one launch (start us, length us, event | category | flops | bytes accessed | tf_op | source)
XLA Modules:
  0.0 51.8 jit_solution(4141286088982023378)
XLA Ops:
  0.6 48.1 %shard_map.77 = (f32[768,128]{1,0:T(8,128)}, f32[8,128]{1,0:T(8,128)}) custom-call(f32[768,128]{1,0:T(8,128)} %start_ref.1, bf16[7,768,256]{2,1,0:T(8,128)(2,1)} %left_hbm.1, bf16[7,768,128]{2,1,0:T(8,128)(2,1)} %right_hbm.1, s32[1,4]{1,0:T(1,128)} %send_hbm.1, s32[3,7]{1,0:T(4,128)} %term_hbm.1, s32[3]{0:T(128)} %len_hbm.1), custom_call_target="tpu_custom_call" | custom-call | tf_op jit(solution)/shard_map/pallas_call | solution.py:383
  48.7 1.3 %slice_reduce_fusion = f32[5]{0:T(128)} fusion(f32[8,128]{1,0:T(8,128)} %get-tuple-element.5), kind=kLoop, calls=%fused_computation | loop fusion | bytes 40 | tf_op jit(solution)/shard_map/slice | solution.py:437
  50.0 1.8 %copy.9 = f32[768,128]{1,0:T(8,128)} copy(f32[768,128]{1,0:T(8,128)} %get-tuple-element.8) | data formatting | bytes 786432

commit v6 on v5

--- a/solution.py
+++ b/solution.py
@@ -166,7 +166,7 @@
         for step in range(1, n_col):
             target = lax.rem(col + step, n_col)
             remote(
-                field, across.at[j, col], across_send.at[j, step], across_recv.at[j, col],
+                half.at[j], across.at[j, col], across_send.at[j, step], across_recv.at[j, col],
                 {"col": target},
             ).start()
 
@@ -239,7 +239,7 @@
                 remote(
                     theirs, theirs, across_send.at[j, step], across_recv.at[j, source], sibling
                 ).wait_recv()
-            overlap = overlap + fold(across[j, source, p] * values[step - 1])
+            overlap = overlap + fold(across[j, source, p].astype(jnp.float32) * values[step - 1])
         return overlap
 
     def add_col(j, p):
@@ -335,7 +335,7 @@
         alpha = overlap * scale * scale
         for step in range(1, n_col):
             remote(
-                field, across.at[j, col], across_send.at[j, step], across_recv.at[j, col], sibling
+                half.at[j], across.at[j, col], across_send.at[j, step], across_recv.at[j, col], sibling
             ).wait_send()
         for p in range(sec_dev):
             v = field[p] * scale
@@ -403,7 +403,7 @@
             pltpu.VMEM((STEPS, sec_dev, n_col, rows, columns), f32),
             pltpu.VMEM((STEPS, sec_dev, n_col, rows, columns), send),
             pltpu.VMEM((STEPS, sec_dev, n_col, rows, columns), send),
-            pltpu.VMEM((STEPS, n_col, sec_dev, rows, columns), f32),
+            pltpu.VMEM((STEPS, n_col, sec_dev, rows, columns), bf),
             pltpu.VMEM((STEPS, team, 2, columns), f32),
             pltpu.VMEM((STEPS, n_row, 2, columns), f32),
             pltpu.VMEM((sec_dev, rows, columns), f32),

time: 52 us -> 52 us (level)
  no operation moved by 1% of the time
where the time goes in v6:
time: 52 us; the launch traced here: 51.8 us
  Pallas kernels  48.1 us (92%)
  local copies, waits for them, and re-layouts  3.07 us (6%)
  between operations  0.64 us (1%)
    pallas_call x1, Pallas kernels, on_device(): pl.pallas_call(functools.partial(kernel, sizes), out_shape=(jax.ShapeDtyp...  48.1 us
    unnamed x1, local copies, waits for them, and re-layouts  1.77 us
    slice x1, local copies, waits for them, and re-layouts, on_device(): return (resid, coef[:2 * STEPS - 1, 0])  1.3 us

profile of v6, /device:TPU:0, one launch (start us, length us, event | category | flops | bytes accessed | tf_op | source)
XLA Modules:
  0.0 51.8 jit_solution(4188329787045420552)
XLA Ops:
  0.6 48.1 %shard_map.77 = (f32[768,128]{1,0:T(8,128)}, f32[8,128]{1,0:T(8,128)}) custom-call(f32[768,128]{1,0:T(8,128)} %start_ref.1, bf16[7,768,256]{2,1,0:T(8,128)(2,1)} %left_hbm.1, bf16[7,768,128]{2,1,0:T(8,128)(2,1)} %right_hbm.1, s32[1,4]{1,0:T(1,128)} %send_hbm.1, s32[3,7]{1,0:T(4,128)} %term_hbm.1, s32[3]{0:T(128)} %len_hbm.1), custom_call_target="tpu_custom_call" | custom-call | tf_op jit(solution)/shard_map/pallas_call | solution.py:383
  48.7 1.3 %slice_reduce_fusion = f32[5]{0:T(128)} fusion(f32[8,128]{1,0:T(8,128)} %get-tuple-element.5), kind=kLoop, calls=%fused_computation | loop fusion | bytes 40 | tf_op jit(solution)/shard_map/slice | solution.py:437
  50.0 1.8 %copy.9 = f32[768,128]{1,0:T(8,128)} copy(f32[768,128]{1,0:T(8,128)} %get-tuple-element.8) | data formatting | bytes 786432
